TPU v7x, 32 devices: a whole 2x2x4 slice. The times are simulated.
32 devices in a mesh: groups: 1, row: 32 (over z, y, x, core), col: 1.
Axes of the slice: x: 2, y: 2, z: 4, core: 2. Of those that a mesh axis runs over, the one named last changes fastest.
Arguments:
- pair: bfloat16 [128, 128, 128], P(('groups', 'row'), 'col'), may hold values from -6 to 6
- token_mask: int32 [128], P('groups'), may hold values 0 or 1
- tri_in_weight: bfloat16 [128, 512], replicated, may hold values from -0.5 to 0.5
- tri_gate_weight: bfloat16 [128, 128], replicated, may hold values from -0.5 to 0.5
- tri_out_weight: bfloat16 [128, 128], replicated, may hold values from -0.5 to 0.5
- atom_act: bfloat16 [2048, 128], P(('groups', 'row')), may hold values from -6 to 6
- atom_cond: bfloat16 [2048, 128], P(('groups', 'row')), may hold values from -60 to 60
- atom_token: int32 [2048], P(('groups', 'row')), may hold values from 0 to 127, as said below
- atom_mask: int32 [2048], P(('groups', 'row')), may hold values from 0 to 1, as said below
- ada_weight: bfloat16 [128, 256], replicated, may hold values from -0.5 to 0.5
- qkv_weight: bfloat16 [128, 384], replicated, may hold values from -0.5 to 0.5
- bias_weight: bfloat16 [128, 4], replicated, may hold values from -0.5 to 0.5
- attn_out_weight: bfloat16 [128, 128], replicated, may hold values from -0.5 to 0.5
- ffn_in_weight: bfloat16 [128, 512], replicated, may hold values from -0.5 to 0.5
- ffn_out_weight: bfloat16 [256, 128], replicated, may hold values from -0.375 to 0.375
- agg_weight: bfloat16 [128, 384], replicated, may hold values from -0.5 to 0.5
Outputs:
- pair_out: bfloat16 [128, 128, 128], P(('groups', 'row'), 'col')
- atom_out: bfloat16 [2048, 128], P(('groups', 'row'))
- token_out: bfloat16 [128, 384], P(('groups', 'row'))
Inputs may be any that keep to these rules, and one draw needn't show every extreme that they name: `atom_token`: Nondecreasing; slots r * 64 to (r + 1) * 64 - 1 hold the atoms of tokens r * 4 to (r + 1) * 4 - 1 followed by padding slots that name the last of those tokens; every token has 1 to 24 atoms. `atom_mask`: in each slab of 64 slots the atoms come first and at most 31 padding slots follow.
All inputs are finite; a program needn't handle non-finite values.
Results may differ from a plain program's by a relative error of at most 0.012.
The roundings to bfloat16 on the way count: a program that leaves them out, or rounds other values in their place, can miss the bound.
Values may be sent and summed in bfloat16 or wider, within the bound.
A program may use at most 64 MiB of HBM per device.

v0:
```python
import math

import jax
import jax.numpy as jnp
from jax import lax
from jax.sharding import PartitionSpec as P

QUERY_WINDOW = 32
KEYS = 128


EPSILON = 1e-05


def extended(shard, sides, width):
    for axis, dim in sides:
        size, length = (lax.axis_size(axis), shard.shape[dim])
        up = [(i, (i + 1) % size) for i in range(size - 1)]
        down = [(j, i) for i, j in up]
        last = lax.slice_in_dim(shard, length - width, length, axis=dim)
        first = lax.slice_in_dim(shard, 0, width, axis=dim)
        before = lax.ppermute(last, axis, up)
        after = lax.ppermute(first, axis, down)
        shard = jnp.concatenate([before, shard, after], axis=dim)
    return shard


def layer_norm(values, along):
    average = jnp.mean(values, axis=along, keepdims=True)
    centred = values - average
    spread = jnp.mean(centred * centred, axis=along, keepdims=True)
    return centred / jnp.sqrt(spread + EPSILON)


def per_device(
    pair,
    token_mask,
    tri_in_weight,
    tri_gate_weight,
    tri_out_weight,
    atom_act,
    atom_cond,
    atom_token,
    atom_mask,
    ada_weight,
    qkv_weight,
    bias_weight,
    attn_out_weight,
    ffn_in_weight,
    ffn_out_weight,
    agg_weight,
):
    tok_rows = pair.shape[0]
    col_count = pair.shape[1]
    channels = pair.shape[2]
    row_index = lax.axis_index("row")
    col_index = lax.axis_index("col")
    pair_float = pair.astype(jnp.float32)
    pair_norm = layer_norm(pair_float, 2).astype(jnp.bfloat16)
    row_live = lax.dynamic_slice_in_dim(token_mask, row_index * tok_rows, tok_rows, 0).astype(
        jnp.float32
    )
    col_live = lax.dynamic_slice_in_dim(token_mask, col_index * col_count, col_count, 0).astype(
        jnp.float32
    )
    pair_live = row_live[:, None] * col_live[None, :]
    left_terms = jnp.einsum(
        "ijd,de->eij",
        pair_norm,
        tri_in_weight[:, : 2 * channels],
        preferred_element_type=jnp.float32,
    )
    left = (jax.nn.sigmoid(left_terms[channels:]) * left_terms[:channels] * pair_live).astype(
        jnp.bfloat16
    )
    right_terms = jnp.einsum(
        "ijd,de->eij",
        pair_norm,
        tri_in_weight[:, 2 * channels :],
        preferred_element_type=jnp.float32,
    )
    right = (jax.nn.sigmoid(right_terms[channels:]) * right_terms[:channels] * pair_live).astype(
        jnp.bfloat16
    )
    tri_gate = jax.nn.sigmoid(
        jnp.einsum("ijd,de->ije", pair_norm, tri_gate_weight, preferred_element_type=jnp.float32)
    )
    left_owned, right_owned = (
        lax.all_to_all(left, "row", split_axis=0, concat_axis=1, tiled=True),
        lax.all_to_all(right, "row", split_axis=0, concat_axis=1, tiled=True),
    )
    left_full, right_rows = (
        lax.all_gather(left_owned, "col", axis=2, tiled=True),
        lax.all_gather(right_owned, "col", axis=2, tiled=True),
    )
    right_used = lax.dynamic_slice_in_dim(right_rows, col_index * col_count, col_count, 1)
    tri_sum = jnp.einsum(
        "cik,cjk->cij", left_full, right_used, preferred_element_type=jnp.float32
    ).astype(jnp.bfloat16)
    merged = lax.all_to_all(tri_sum, "row", split_axis=1, concat_axis=0, tiled=True)
    tri_norm = layer_norm(merged.astype(jnp.float32), 0).astype(jnp.bfloat16)
    update = jnp.einsum("dij,de->ije", tri_norm, tri_out_weight, preferred_element_type=jnp.float32)
    pair_out = (pair_float + tri_gate * update).astype(jnp.bfloat16)
    band_width = 3 * tok_rows
    targets = (row_index - 1) * tok_rows + jnp.arange(band_width, dtype=jnp.int32)
    columns = col_index * col_count + jnp.arange(col_count, dtype=jnp.int32)
    selector = (columns[:, None] == targets[None, :]).astype(jnp.bfloat16)
    band_part = jnp.einsum("ijd,jb->ibd", pair_out, selector, preferred_element_type=jnp.float32)
    band = lax.psum(band_part.astype(jnp.bfloat16), "col").astype(jnp.float32)
    band_norm = layer_norm(band, 2).astype(jnp.bfloat16)
    bias_table = jnp.einsum(
        "ibd,dh->ibh", band_norm, bias_weight, preferred_element_type=jnp.float32
    ).astype(jnp.bfloat16)
    slab = atom_act.shape[0]
    window_width = atom_act.shape[1]
    heads = bias_weight.shape[1]
    head_size = window_width // heads
    side = (KEYS - QUERY_WINDOW) // 2
    windows = slab // QUERY_WINDOW
    local_token = atom_token - row_index * tok_rows
    live = atom_mask.astype(jnp.float32)
    token_tag = ((local_token + 1) * atom_mask).astype(jnp.bfloat16)
    ada = jnp.dot(atom_cond, ada_weight, preferred_element_type=jnp.float32)
    atom_inputs = (
        jax.nn.sigmoid(ada[:, :window_width]) * layer_norm(atom_act.astype(jnp.float32), 1)
        + ada[:, window_width:]
    ).astype(jnp.bfloat16)
    projected = jnp.dot(atom_inputs, qkv_weight, preferred_element_type=jnp.float32).astype(
        jnp.bfloat16
    )
    queries = projected[:, :window_width]
    ext_pairs, ext_tag = (
        extended(projected[:, window_width:], (("row", 0),), side),
        extended(token_tag, (("row", 0),), side),
    )
    ext_rows = slab + 2 * side
    ext_position = jnp.arange(ext_rows, dtype=jnp.int32)
    offset = jnp.where(
        ext_position < side, 0, jnp.where(ext_position < side + slab, tok_rows, 2 * tok_rows)
    )
    tag_value = ext_tag.astype(jnp.int32)
    key_valid = tag_value > 0
    band_index = tag_value - 1 + offset
    band_slots = jnp.arange(band_width, dtype=jnp.int32)
    key_onehot = ((band_index[:, None] == band_slots[None, :]) & key_valid[:, None]).astype(
        jnp.bfloat16
    )
    query_onehot = (local_token[:, None] == jnp.arange(tok_rows, dtype=jnp.int32)[None, :]).astype(
        jnp.bfloat16
    )
    query_bias = jnp.einsum(
        "lt,tbh->lbh", query_onehot, bias_table, preferred_element_type=jnp.float32
    ).astype(jnp.bfloat16)
    query_bias = query_bias.reshape(windows, QUERY_WINDOW, band_width, heads)
    key_index = (
        jnp.arange(windows, dtype=jnp.int32)[:, None] * QUERY_WINDOW
        + jnp.arange(KEYS, dtype=jnp.int32)[None, :]
    )
    window_pairs = ext_pairs[key_index]
    window_onehot = key_onehot[key_index]
    window_valid = key_valid[key_index]
    window_bias = jnp.einsum(
        "wlbh,wmb->whlm", query_bias, window_onehot, preferred_element_type=jnp.float32
    )
    query_heads = queries.reshape(windows, QUERY_WINDOW, heads, head_size)
    key_heads = window_pairs[..., :window_width].reshape(windows, KEYS, heads, head_size)
    value_heads = window_pairs[..., window_width:].reshape(windows, KEYS, heads, head_size)
    logit_scores = (
        jnp.einsum("wlhd,wmhd->whlm", query_heads, key_heads, preferred_element_type=jnp.float32)
        / math.sqrt(head_size)
        + window_bias
    )
    logit_scores = jnp.where(window_valid[:, None, None, :], logit_scores, -1e30)
    attn_weights = jax.nn.softmax(logit_scores, axis=-1).astype(jnp.bfloat16)
    attended = (
        jnp.einsum("whlm,wmhd->wlhd", attn_weights, value_heads, preferred_element_type=jnp.float32)
        .reshape(slab, window_width)
        .astype(jnp.bfloat16)
    )
    atom_mid = atom_act.astype(jnp.float32) + jnp.dot(
        attended, attn_out_weight, preferred_element_type=jnp.float32
    )
    atom_norm = layer_norm(atom_mid, 1).astype(jnp.bfloat16)
    expanded = jnp.dot(atom_norm, ffn_in_weight, preferred_element_type=jnp.float32)
    hidden_width = ffn_out_weight.shape[0]
    inner = (jax.nn.silu(expanded[:, :hidden_width]) * expanded[:, hidden_width:]).astype(
        jnp.bfloat16
    )
    atom_out = (
        (atom_mid + jnp.dot(inner, ffn_out_weight, preferred_element_type=jnp.float32))
        * live[:, None]
    ).astype(jnp.bfloat16)
    features = jax.nn.relu(
        jnp.dot(atom_out, agg_weight, preferred_element_type=jnp.float32)
    ).astype(jnp.bfloat16)
    live_onehot = query_onehot * atom_mask.astype(jnp.bfloat16)[:, None]
    token_sums = jnp.einsum("at,ac->tc", live_onehot, features, preferred_element_type=jnp.float32)
    token_counts = jnp.sum(live_onehot.astype(jnp.float32), axis=0)
    token_out = (token_sums / token_counts[:, None]).astype(jnp.bfloat16)
    return (pair_out, atom_out, token_out)


def solution(mesh):
    in_specs = (
        P(("groups", "row"), "col", None),
        P("groups"),
        P(),
        P(),
        P(),
        P(("groups", "row"), None),
        P(("groups", "row"), None),
        P(("groups", "row")),
        P(("groups", "row")),
        P(),
        P(),
        P(),
        P(),
        P(),
        P(),
        P(),
    )
    out_specs = (
        P(("groups", "row"), "col", None),
        P(("groups", "row"), None),
        P(("groups", "row"), None),
    )
    return jax.shard_map(
        per_device, mesh=mesh, in_specs=in_specs, out_specs=out_specs, check_vma=False
    )
```

profile of v0, /device:TPU:0, one launch (start us, length us, event | category | flops | bytes accessed | tf_op | source)
XLA Modules:
  0.0 61.1 jit_solution(8596969497097267078)
XLA Ops:
  0.7 1.1 %convert_reduce_fusion = f32[4,128]{1,0:T(4,128)S(1)} fusion(bf16[4,128,128]{2,1,0:T(8,128)(2,1)} %param.16), kind=kLoop, calls=%fused_computation.38 | loop fusion | flops 130560 | bytes 133120 | tf_op jit(solution)/shard_map/reduce_sum | solution.py:29
  2.7 0.6 %copy-done.17 = s32[128]{0:T(128)S(1)} copy-done((s32[128]{0:T(128)S(1)}, s32[128]{0:T(128)}, u32[]{:S(2)}) %copy-start.17) | copy-done | bytes 536
  3.7 0.8 %copy.43 = bf16[128,4,128]{2,1,0:T(4,128)(2,1)} copy(bf16[128,4,128]{0,2,1:T(8,128)(2,1)S(1)} %get-tuple-element.11) | data formatting | bytes 262144 | tf_op jit(solution)/shard_map/convert_element_type | solution.py:82
  4.5 7.3 %all-to-all-start.1 = ((bf16[128,4,128]{2,1,0:T(4,128)(2,1)}), bf16[128,4,128]{2,1,0:T(4,128)(2,1)S(1)}, u32[]{:S(2)}, u32[]{:S(2)}) async-start(bf16[128,4,128]{2,1,0:T(4,128)(2,1)} %copy.43), calls=%async_computation.1 | async-start | bytes 262144 | tf_op jit(solution)/shard_map/all_to_all | solution.py:90
  11.9 2.1 %collective-permute-start.2 = (bf16[48]{0:T(256)(128)(2,1)S(1)}, bf16[48]{0:T(256)(128)(2,1)S(1)}, u32[]{:S(2)}, u32[]{:S(2)}) collective-permute-start(bf16[48]{0:T(256)(128)(2,1)S(1)} %get-tuple-element.15), channel_id=1, source_target_pairs={{0,1},{1,2},{2,3},{3,4},{4,5},{5,6},{6,7},{7,8},{8,9},{9,10},{10,1... | collective-permute-start | bytes 296 | tf_op jit(solution)/shard_map/ppermute | solution.py:22
  14.1 1.3 %collective-permute-start.3 = (bf16[48]{0:T(256)(128)(2,1)S(1)}, bf16[48]{0:T(256)(128)(2,1)S(1)}, u32[]{:S(2)}, u32[]{:S(2)}) collective-permute-start(bf16[48]{0:T(256)(128)(2,1)S(1)} %get-tuple-element.16), channel_id=1, source_target_pairs={{1,0},{2,1},{3,2},{4,3},{5,4},{6,5},{7,6},{8,7},{9,8},{10,9},{11,1... | collective-permute-start | bytes 296 | tf_op jit(solution)/shard_map/ppermute | solution.py:23
  16.1 4.2 %collective-permute-start = (bf16[48,256]{1,0:T(8,128)(2,1)S(1)}, bf16[48,256]{1,0:T(8,128)(2,1)S(1)}, u32[]{:S(2)}, u32[]{:S(2)}) collective-permute-start(bf16[48,256]{1,0:T(8,128)(2,1)S(1)} %get-tuple-element.9), channel_id=1, source_target_pairs={{0,1},{1,2},{2,3},{3,4},{4,5},{5,6},{6,7},{7,8},{8,9},{9,10},{10,1... | collective-permute-start | bytes 73736 | tf_op jit(solution)/shard_map/ppermute | solution.py:22
  20.3 1.3 %collective-permute-start.1 = (bf16[48,256]{1,0:T(8,128)(2,1)S(1)}, bf16[48,256]{1,0:T(8,128)(2,1)S(1)}, u32[]{:S(2)}, u32[]{:S(2)}) collective-permute-start(bf16[48,256]{1,0:T(8,128)(2,1)S(1)} %get-tuple-element.10), channel_id=1, source_target_pairs={{1,0},{2,1},{3,2},{4,3},{5,4},{6,5},{7,6},{8,7},{9,8},{10,9},{11,1... | collective-permute-start | bytes 73736 | tf_op jit(solution)/shard_map/ppermute | solution.py:23
  22.0 0.8 %copy.40 = bf16[128,4,128]{2,1,0:T(4,128)(2,1)} copy(bf16[128,4,128]{0,2,1:T(8,128)(2,1)S(1)} %get-tuple-element.12) | data formatting | bytes 262144 | tf_op jit(solution)/shard_map/convert_element_type | solution.py:73
  23.2 9.8 %all-to-all-start = ((bf16[128,4,128]{2,1,0:T(4,128)(2,1)}), bf16[128,4,128]{2,1,0:T(4,128)(2,1)S(1)}, u32[]{:S(2)}, u32[]{:S(2)}) async-start(bf16[128,4,128]{2,1,0:T(4,128)(2,1)} %copy.40), calls=%async_computation | async-start | bytes 262144 | tf_op jit(solution)/shard_map/all_to_all | solution.py:89
  33.0 1.9 %gather_fusion.1 = pred[256]{0:T(512)(128)(4,1)S(1)} fusion(pred[160]{0:T(512)(128)(4,1)S(1)} %get-tuple-element.3, s32[1024]{0:T(1024)S(1)} %pad_clamp_fusion), kind=kCustom, calls=%fused_computation.1 | custom fusion | bytes 1536 | tf_op jit(solution)/shard_map/gather | solution.py:161
  35.0 0.8 %gather_fusion.2 = pred[256,12]{1,0:T(32,128)(4,1)S(1)} fusion(pred[160,12]{1,0:T(8,128)(4,1)S(1)} %fusion.37, s32[1024]{0:T(1024)S(1)} %pad_clamp_fusion), kind=kCustom, calls=%fused_computation.2 | custom fusion | bytes 7168 | tf_op jit(solution)/shard_map/gather | solution.py:160
  35.9 5.3 %all-to-all-done = bf16[128,4,128]{2,1,0:T(4,128)(2,1)S(1)} async-done(((bf16[128,4,128]{2,1,0:T(4,128)(2,1)}), bf16[128,4,128]{2,1,0:T(4,128)(2,1)S(1)}, u32[]{:S(2)}, u32[]{:S(2)}) %all-to-all-start) | async-done | bytes 131104 | tf_op jit(solution)/shard_map/all_to_all | solution.py:89
  41.5 0.8 %copy.46 = bf16[4,128,128]{2,0,1:T(4,128)(2,1)} copy(bf16[4,128,128]{2,1,0:T(8,128)(2,1)S(1)} %convolution_convert_fusion) | data formatting | bytes 262144 | tf_op jit(solution)/shard_map/convert_element_type | solution.py:99
  42.3 2.7 %all-to-all-start.2 = ((bf16[4,128,128]{2,0,1:T(4,128)(2,1)}), bf16[4,128,128]{2,0,1:T(4,128)(2,1)S(1)}, u32[]{:S(2)}, u32[]{:S(2)}) async-start(bf16[4,128,128]{2,0,1:T(4,128)(2,1)} %copy.46), calls=%async_computation.2 | async-start | bytes 262144 | tf_op jit(solution)/shard_map/all_to_all | solution.py:100
  45.1 1.2 %gather_fusion = bf16[256,256]{1,0:T(8,128)(2,1)S(1)} fusion(bf16[160,256]{1,0:T(8,128)(2,1)S(1)} %pad_maximum_fusion, s32[1024]{0:T(1024)S(1)} %pad_clamp_fusion), kind=kCustom, calls=%fused_computation | custom fusion | bytes 263168 | tf_op jit(solution)/shard_map/gather | solution.py:159
  46.5 6.7 %all-to-all-done.2 = bf16[4,128,128]{2,0,1:T(4,128)(2,1)S(1)} async-done(((bf16[4,128,128]{2,0,1:T(4,128)(2,1)}), bf16[4,128,128]{2,0,1:T(4,128)(2,1)S(1)}, u32[]{:S(2)}, u32[]{:S(2)}) %all-to-all-start.2) | async-done | bytes 131104 | tf_op jit(solution)/shard_map/all_to_all | solution.py:100
  53.5 0.7 %copy-done.15 = bf16[128,128]{1,0:T(8,128)(2,1)S(1)} copy-done((bf16[128,128]{1,0:T(8,128)(2,1)S(1)}, bf16[128,128]{1,0:T(8,128)(2,1)}, u32[]{:S(2)}) %copy-start.15) | copy-done | bytes 32792
  54.9 0.7 %copy-done.16 = bf16[128,4]{0,1:T(4,128)(2,1)S(1)} copy-done((bf16[128,4]{0,1:T(4,128)(2,1)S(1)}, bf16[128,4]{0,1:T(4,128)(2,1)}, u32[]{:S(2)}) %copy-start.16) | copy-done | bytes 1048
  56.7 0.5 fusion.11
  57.4 0.6 %copy-done.6 = bf16[128,128]{1,0:T(8,128)(2,1)S(1)} copy-done((bf16[128,128]{1,0:T(8,128)(2,1)S(1)}, bf16[128,128]{1,0:T(8,128)(2,1)}, u32[]{:S(2)}) %copy-start.6) | copy-done | bytes 32792
  58.7 0.6 %copy-done.13 = bf16[256,128]{1,0:T(8,128)(2,1)S(1)} copy-done((bf16[256,128]{1,0:T(8,128)(2,1)S(1)}, bf16[256,128]{1,0:T(8,128)(2,1)}, u32[]{:S(2)}) %copy-start.13) | copy-done | bytes 65560
  59.5 0.7 %copy-done.12 = bf16[128,384]{1,0:T(8,128)(2,1)S(1)} copy-done((bf16[128,384]{1,0:T(8,128)(2,1)S(1)}, bf16[128,384]{1,0:T(8,128)(2,1)}, u32[]{:S(2)}) %copy-start.12) | copy-done | bytes 98328
  60.3 0.8 %fusion.18 = bf16[4,384]{1,0:T(4,128)(2,1)} fusion(bf16[64,128]{1,0:T(8,128)(2,1)S(1)} %fusion.14, bf16[128,384]{1,0:T(8,128)(2,1)S(1)} %copy-done.12, f32[4]{0:T(128)S(1)} %convert_reduce_fusion.2, s32[64]{0:T(128)S(1)} %get-tuple-element.6, bf16[64]{0:T(256)(128)(2,1)S(1)} %get-tuple-element.13), kind=kOutput, calls=%fused_computation.36 | convolution fusion | flops 6540800 | bytes 118160 | tf_op jit(solution)/shard_map/at,ac->tc/dot_general | solution.py:197
  (103 shorter events, 6.5 us)
Async XLA Ops:
  0.6 57.9 %copy-start = (bf16[128,512]{1,0:T(8,128)(2,1)S(1)}, bf16[128,512]{1,0:T(8,128)(2,1)}, u32[]{:S(2)}) copy-start(bf16[128,512]{1,0:T(8,128)(2,1)} %param.29) | copy-start | bytes 393220
  0.6 1.1 %copy-start.1 = (bf16[4,128,128]{2,1,0:T(8,128)(2,1)S(1)}, bf16[4,128,128]{2,1,0:T(8,128)(2,1)}, u32[]{:S(2)}) copy-start(bf16[4,128,128]{2,1,0:T(8,128)(2,1)} %param.16) | copy-start | bytes 393220
  0.7 1.4 %copy-start.10 = (bf16[128,512]{1,0:T(8,128)(2,1)S(1)}, bf16[128,512]{1,0:T(8,128)(2,1)}, u32[]{:S(2)}) copy-start(bf16[128,512]{1,0:T(8,128)(2,1)} %param.18) | copy-start | bytes 393220
  4.4 7.3 %copy-start.8 = (s32[64]{0:T(128)S(1)}, s32[64]{0:T(128)}, u32[]{:S(2)}) copy-start(s32[64]{0:T(128)} %param.24) | copy-start | bytes 772
  4.4 7.3 %copy-start.9 = (s32[64]{0:T(128)S(1)}, s32[64]{0:T(128)}, u32[]{:S(2)}) copy-start(s32[64]{0:T(128)} %param.23) | copy-start | bytes 772
  4.5 10.9 %copy-start.3 = (bf16[64,128]{1,0:T(8,128)(2,1)S(1)}, bf16[64,128]{1,0:T(8,128)(2,1)}, u32[]{:S(2)}) copy-start(bf16[64,128]{1,0:T(8,128)(2,1)} %param.21) | copy-start | bytes 49156
  4.5 11.2 %copy-start.5 = (bf16[128,256]{1,0:T(8,128)(2,1)S(1)}, bf16[128,256]{1,0:T(8,128)(2,1)}, u32[]{:S(2)}) copy-start(bf16[128,256]{1,0:T(8,128)(2,1)} %param.25) | copy-start | bytes 196612
  4.5 11.4 %copy-start.11 = (bf16[128,384]{1,0:T(8,128)(2,1)S(1)}, bf16[128,384]{1,0:T(8,128)(2,1)}, u32[]{:S(2)}) copy-start(bf16[128,384]{1,0:T(8,128)(2,1)} %param.26) | copy-start | bytes 294916
  4.5 18.7 %all-to-all-start.1 = ((bf16[128,4,128]{2,1,0:T(4,128)(2,1)}), bf16[128,4,128]{2,1,0:T(4,128)(2,1)S(1)}, u32[]{:S(2)}, u32[]{:S(2)}) async-start(bf16[128,4,128]{2,1,0:T(4,128)(2,1)} %copy.43), calls=%async_computation.1 | async-start | bytes 262144 | tf_op jit(solution)/shard_map/all_to_all | solution.py:90
  11.9 11.2 %collective-permute-start.2 = (bf16[48]{0:T(256)(128)(2,1)S(1)}, bf16[48]{0:T(256)(128)(2,1)S(1)}, u32[]{:S(2)}, u32[]{:S(2)}) collective-permute-start(bf16[48]{0:T(256)(128)(2,1)S(1)} %get-tuple-element.15), channel_id=1, source_target_pairs={{0,1},{1,2},{2,3},{3,4},{4,5},{5,6},{6,7},{7,8},{8,9},{9,10},{10,1... | collective-permute-start | bytes 296 | tf_op jit(solution)/shard_map/ppermute | solution.py:22
  14.0 1.6 %copy-start.7 = (bf16[64,128]{1,0:T(8,128)(2,1)S(1)}, bf16[64,128]{1,0:T(8,128)(2,1)}, u32[]{:S(2)}) copy-start(bf16[64,128]{1,0:T(8,128)(2,1)} %param.22) | copy-start | bytes 49156
  14.1 9.0 %collective-permute-start.3 = (bf16[48]{0:T(256)(128)(2,1)S(1)}, bf16[48]{0:T(256)(128)(2,1)S(1)}, u32[]{:S(2)}, u32[]{:S(2)}) collective-permute-start(bf16[48]{0:T(256)(128)(2,1)S(1)} %get-tuple-element.16), channel_id=1, source_target_pairs={{1,0},{2,1},{3,2},{4,3},{5,4},{6,5},{7,6},{8,7},{9,8},{10,9},{11,1... | collective-permute-start | bytes 296 | tf_op jit(solution)/shard_map/ppermute | solution.py:23
  16.1 6.0 %copy-start.2 = (bf16[64,384]{1,0:T(8,128)(2,1)}, bf16[64,384]{1,0:T(8,128)(2,1)S(1)}, u32[]{:S(2)}) copy-start(bf16[64,384]{1,0:T(8,128)(2,1)S(1)} %convolution_convert_fusion.2) | copy-start | bytes 147460
  16.1 5.5 %copy-start.14 = (bf16[128,128]{1,0:T(8,128)(2,1)S(1)}, bf16[128,128]{1,0:T(8,128)(2,1)}, u32[]{:S(2)}) copy-start(bf16[128,128]{1,0:T(8,128)(2,1)} %param.19) | copy-start | bytes 98308
  16.1 28.9 %collective-permute-start = (bf16[48,256]{1,0:T(8,128)(2,1)S(1)}, bf16[48,256]{1,0:T(8,128)(2,1)S(1)}, u32[]{:S(2)}, u32[]{:S(2)}) collective-permute-start(bf16[48,256]{1,0:T(8,128)(2,1)S(1)} %get-tuple-element.9), channel_id=1, source_target_pairs={{0,1},{1,2},{2,3},{3,4},{4,5},{5,6},{6,7},{7,8},{8,9},{9,10},{10,1... | collective-permute-start | bytes 73736 | tf_op jit(solution)/shard_map/ppermute | solution.py:22
  20.3 24.8 %collective-permute-start.1 = (bf16[48,256]{1,0:T(8,128)(2,1)S(1)}, bf16[48,256]{1,0:T(8,128)(2,1)S(1)}, u32[]{:S(2)}, u32[]{:S(2)}) collective-permute-start(bf16[48,256]{1,0:T(8,128)(2,1)S(1)} %get-tuple-element.10), channel_id=1, source_target_pairs={{1,0},{2,1},{3,2},{4,3},{5,4},{6,5},{7,6},{8,7},{9,8},{10,9},{11,1... | collective-permute-start | bytes 73736 | tf_op jit(solution)/shard_map/ppermute | solution.py:23
  22.0 0.9 %slice-start.1 = ((bf16[64,384]{1,0:T(8,128)(2,1)}), bf16[64,128]{1,0:T(8,128)(2,1)S(1)}, s32[]{:S(2)}) async-start(bf16[64,384]{1,0:T(8,128)(2,1)} %copy-done.2), calls=%async_computation.4 | async-start | bytes 32768 | tf_op jit(solution)/shard_map/slice | solution.py:131
  23.2 18.0 %all-to-all-start = ((bf16[128,4,128]{2,1,0:T(4,128)(2,1)}), bf16[128,4,128]{2,1,0:T(4,128)(2,1)S(1)}, u32[]{:S(2)}, u32[]{:S(2)}) async-start(bf16[128,4,128]{2,1,0:T(4,128)(2,1)} %copy.40), calls=%async_computation | async-start | bytes 262144 | tf_op jit(solution)/shard_map/all_to_all | solution.py:89
  42.3 2.7 %slice-start = ((bf16[64,384]{1,0:T(8,128)(2,1)}), bf16[64,256]{1,0:T(8,128)(2,1)S(1)}, s32[]{:S(2)}) async-start(bf16[64,384]{1,0:T(8,128)(2,1)} %copy-done.2), calls=%async_computation.3 | async-start | bytes 65536 | tf_op jit(solution)/shard_map/slice | solution.py:133
  42.3 10.9 %all-to-all-start.2 = ((bf16[4,128,128]{2,0,1:T(4,128)(2,1)}), bf16[4,128,128]{2,0,1:T(4,128)(2,1)S(1)}, u32[]{:S(2)}, u32[]{:S(2)}) async-start(bf16[4,128,128]{2,0,1:T(4,128)(2,1)} %copy.46), calls=%async_computation.2 | async-start | bytes 262144 | tf_op jit(solution)/shard_map/all_to_all | solution.py:100
  54.4 1.4 %copy-start.4 = (bf16[4,128,128]{2,1,0:T(8,128)(2,1)}, bf16[4,128,128]{2,1,0:T(8,128)(2,1)S(1)}, u32[]{:S(2)}) copy-start(bf16[4,128,128]{2,1,0:T(8,128)(2,1)S(1)} %fusion.5) | copy-start | bytes 393220
  58.5 0.8 %copy-start.13 = (bf16[256,128]{1,0:T(8,128)(2,1)S(1)}, bf16[256,128]{1,0:T(8,128)(2,1)}, u32[]{:S(2)}) copy-start(bf16[256,128]{1,0:T(8,128)(2,1)} %param.30) | copy-start | bytes 196612
  59.4 0.9 %copy-start.12 = (bf16[128,384]{1,0:T(8,128)(2,1)S(1)}, bf16[128,384]{1,0:T(8,128)(2,1)}, u32[]{:S(2)}) copy-start(bf16[128,384]{1,0:T(8,128)(2,1)} %param.31) | copy-start | bytes 294916
  60.2 0.9 %copy-start.18 = (bf16[64,128]{1,0:T(8,128)(2,1)}, bf16[64,128]{1,0:T(8,128)(2,1)S(1)}, u32[]{:S(2)}) copy-start(bf16[64,128]{1,0:T(8,128)(2,1)S(1)} %fusion.14) | copy-start | bytes 49156
  (4 other events, 2.9 us)
where the time goes:
time: 61.9 us; the launch traced here: 61.1 us
  starting transfers between devices  28.7 us (46%)
  waiting for transfers between devices  12 us (19%)
  local copies, waits for them, and re-layouts  11.3 us (18%)
  matrix products  4.74 us (8%)
  other arithmetic  3.08 us (5%)
  between operations  1.23 us (2%)
    all_to_all x1, starting transfers between devices, per_device(): lax.all_to_all(left, 'row', split_axis=0, concat_axis=1, tiled=True)  9.8 us
    all_to_all x1, starting transfers between devices, per_device(): lax.all_to_all(right, 'row', split_axis=0, concat_axis=1, tiled=True)  7.3 us
    all_to_all x1, waiting for transfers between devices, per_device(): lax.all_to_all(tri_sum, 'row', split_axis=1, concat_axis=0, tiled=True)  6.74 us
    ppermute x2, starting transfers between devices, extended(): before = lax.ppermute(last, axis, up)  6.31 us
    all_to_all x1, waiting for transfers between devices, per_device(): lax.all_to_all(left, 'row', split_axis=0, concat_axis=1, tiled=True)  5.27 us
    unnamed x40, local copies, waits for them, and re-layouts  4.36 us
    all_to_all x1, starting transfers between devices, per_device(): lax.all_to_all(tri_sum, 'row', split_axis=1, concat_axis=0, tiled=True)  2.71 us
    ppermute x2, starting transfers between devices, extended(): after = lax.ppermute(first, axis, down)  2.58 us
  transfers between devices with their start and end apart: 7, of which 2 were waited for; matrix products, arithmetic and copies ran while one was open for 13% of the time, Pallas kernels for 0%

commit v1 on v0

--- a/solution.py
+++ b/solution.py
@@ -1,8 +1,11 @@
+import functools
 import math
 
 import jax
 import jax.numpy as jnp
 from jax import lax
+from jax.experimental import pallas as pl
+from jax.experimental.pallas import tpu as pltpu
 from jax.sharding import PartitionSpec as P
 
 QUERY_WINDOW = 32
@@ -32,7 +35,7 @@
     return centred / jnp.sqrt(spread + EPSILON)
 
 
-def per_device(
+def spread_device(
     pair,
     token_mask,
     tri_in_weight,
@@ -200,6 +203,364 @@
     return (pair_out, atom_out, token_out)
 
 
+MESH = pl.DeviceIdType.MESH
+F32 = jnp.float32
+BF16 = jnp.bfloat16
+
+
+def dot_nn(a, b):
+    return lax.dot_general(a, b, (((1,), (0,)), ((), ())), preferred_element_type=F32)
+
+
+def dot_nt(a, b):
+    return lax.dot_general(a, b, (((1,), (1,)), ((), ())), preferred_element_type=F32)
+
+
+def dot_tn(a, b):
+    return lax.dot_general(a, b, (((0,), (0,)), ((), ())), preferred_element_type=F32)
+
+
+def normed(values, along):
+    average = jnp.mean(values, axis=along, keepdims=True)
+    centred = values - average
+    spread = jnp.mean(centred * centred, axis=along, keepdims=True)
+    return centred * lax.rsqrt(spread + EPSILON)
+
+
+def fused_kernel(
+    sizes,
+    pair,
+    token_mask,
+    tri_in_weight,
+    tri_gate_weight,
+    tri_out_weight,
+    atom_act,
+    atom_cond,
+    atom_token,
+    atom_mask,
+    ada_weight,
+    qkv_weight,
+    bias_weight,
+    attn_out_weight,
+    ffn_in_weight,
+    ffn_out_weight,
+    agg_weight,
+    pair_out,
+    atom_out,
+    token_out,
+    terms_wide,
+    send_terms,
+    recv_terms,
+    left_wide,
+    right_wide,
+    sums_wide,
+    send_sums,
+    recv_sums,
+    gate_ref,
+    rim,
+    send_sem,
+    recv_sem,
+    rim_send,
+    rim_recv,
+):
+    devices, tok_rows, tokens, channels, owned, slab, heads = sizes
+    block = tok_rows * owned
+    side = (KEYS - QUERY_WINDOW) // 2
+    ext = slab + 2 * side
+    group = lax.axis_index("groups")
+    me = lax.axis_index("row")
+    col = lax.axis_index("col")
+
+    barrier = pltpu.get_barrier_semaphore()
+
+    def greet(step, carry):
+        peer = lax.rem(me + step, devices)
+        pl.semaphore_signal(barrier, inc=1, device_id=(group, peer, col), device_id_type=MESH)
+        return carry
+
+    lax.fori_loop(1, devices, greet, 0)
+
+    mask_row = token_mask[...].astype(F32)
+    lane = lax.broadcasted_iota(jnp.int32, (1, tokens), 1)
+    in_weight = tri_in_weight[...].T
+    for i in range(tok_rows):
+        norm = normed(pair[i].astype(F32), 1).astype(BF16)
+        row_mask = jnp.sum(jnp.where(lane == me * tok_rows + i, mask_row, 0.0), axis=1, keepdims=True)
+        both = row_mask * mask_row
+        terms = dot_nt(in_weight, norm)
+        for part in range(2):
+            base = part * 2 * channels
+            value = (
+                jax.nn.sigmoid(terms[base + channels : base + 2 * channels])
+                * terms[base : base + channels]
+                * both
+            )
+            for c in range(owned):
+                terms_wide[part, pl.ds(i * owned + c, devices, stride=block), :] = value[
+                    c * devices : (c + 1) * devices
+                ]
+        gate_ref[i] = jax.nn.sigmoid(dot_nn(norm, tri_gate_weight[...]))
+    for part in range(2):
+        send_terms[:, part] = terms_wide[part].reshape(devices, block, tokens).astype(BF16)
+
+    pl.semaphore_wait(barrier, devices - 1)
+
+    def terms_copy(peer):
+        return pltpu.make_async_remote_copy(
+            src_ref=send_terms.at[peer],
+            dst_ref=recv_terms.at[me],
+            send_sem=send_sem.at[0],
+            recv_sem=recv_sem.at[0],
+            device_id=(group, peer, col),
+            device_id_type=MESH,
+        )
+
+    def send_first(step, carry):
+        terms_copy(lax.rem(me + step, devices)).start()
+        return carry
+
+    lax.fori_loop(1, devices, send_first, 0)
+    recv_terms[me] = send_terms[me]
+
+    token_row = atom_token[...] - me * tok_rows
+    live_row = atom_mask[...]
+    wide = (channels, slab)
+    token_col = jnp.broadcast_to(token_row.astype(F32), wide).T
+    live_col = jnp.broadcast_to(live_row.astype(F32), wide).T
+    act = atom_act[...].astype(F32)
+    ada = dot_nn(atom_cond[...], ada_weight[...])
+    width = act.shape[1]
+    atom_inputs = (jax.nn.sigmoid(ada[:, :width]) * normed(act, 1) + ada[:, width:]).astype(BF16)
+    projected = dot_nn(atom_inputs, qkv_weight[...]).astype(BF16)
+    rim[side : side + slab, : 2 * width] = projected[:, width:]
+    rim[side : side + slab, 2 * width :] = ((token_col + 1.0) * live_col).astype(BF16)
+
+    up = pltpu.make_async_remote_copy(
+        src_ref=rim.at[pl.ds(slab, side)],
+        dst_ref=rim.at[pl.ds(0, side)],
+        send_sem=rim_send.at[0],
+        recv_sem=rim_recv.at[0],
+        device_id=(group, lax.rem(me + 1, devices), col),
+        device_id_type=MESH,
+    )
+    down = pltpu.make_async_remote_copy(
+        src_ref=rim.at[pl.ds(side, side)],
+        dst_ref=rim.at[pl.ds(side + slab, side)],
+        send_sem=rim_send.at[1],
+        recv_sem=rim_recv.at[1],
+        device_id=(group, lax.rem(me + devices - 1, devices), col),
+        device_id_type=MESH,
+    )
+
+    @pl.when(me < devices - 1)
+    def _():
+        up.start()
+
+    @pl.when(me > 0)
+    def _():
+        down.start()
+
+    @pl.when(me == 0)
+    def _():
+        rim[:side] = jnp.zeros((side, rim.shape[1]), BF16)
+
+    @pl.when(me == devices - 1)
+    def _():
+        rim[side + slab :] = jnp.zeros((side, rim.shape[1]), BF16)
+
+    others = pl.ds(0, devices - 1)
+    pltpu.make_async_copy(send_terms.at[others], recv_terms.at[others], recv_sem.at[0]).wait()
+    left_wide[...] = recv_terms[:, 0].reshape(devices * block, tokens).astype(F32)
+    right_wide[...] = recv_terms[:, 1].reshape(devices * block, tokens).astype(F32)
+    for c in range(owned):
+        rows = pl.ds(c, tokens, stride=owned)
+        sums_wide[rows, :] = dot_nt(
+            left_wide[rows, :].astype(BF16), right_wide[rows, :].astype(BF16)
+        )
+    send_sums[...] = sums_wide[...].reshape(devices, block, tokens).astype(BF16)
+
+    def sums_copy(peer):
+        return pltpu.make_async_remote_copy(
+            src_ref=send_sums.at[peer],
+            dst_ref=recv_sums.at[me],
+            send_sem=send_sem.at[1],
+            recv_sem=recv_sem.at[1],
+            device_id=(group, peer, col),
+            device_id_type=MESH,
+        )
+
+    def send_second(step, carry):
+        sums_copy(lax.rem(me + step, devices)).start()
+        return carry
+
+    lax.fori_loop(1, devices, send_second, 0)
+    recv_sums[me] = send_sums[me]
+
+    @pl.when(me > 0)
+    def _():
+        up.wait_recv()
+
+    @pl.when(me < devices - 1)
+    def _():
+        down.wait_recv()
+
+    head_size = width // heads
+    keys = rim[:, :width]
+    values = rim[:, width : 2 * width]
+    tag = rim[:, 2 * width :].astype(F32)
+    head_lane = lax.broadcasted_iota(jnp.int32, (slab, width), 1) // head_size
+    queries = projected[:, :width].astype(F32)
+    split_queries = jnp.concatenate(
+        [jnp.where(head_lane == h, queries, 0.0) for h in range(heads)], axis=0
+    ).astype(BF16)
+    raw_scores = dot_nt(split_queries, keys) * (1.0 / math.sqrt(head_size))
+    band = 4 * tok_rows
+    dead_lane = tok_rows * band
+    ext_row = lax.broadcasted_iota(jnp.int32, (ext, channels), 0)
+    ext_lane = lax.broadcasted_iota(jnp.int32, (ext, channels), 1)
+    offset = jnp.where(
+        ext_row < side, 0, jnp.where(ext_row < side + slab, tok_rows, 2 * tok_rows)
+    )
+    band_index = tag.astype(jnp.int32) - 1 + offset
+    slot = lax.rem(ext_lane, band)
+    alive = tag > 0.0
+    key_map = jnp.where(
+        ext_lane < dead_lane,
+        jnp.where(alive & (band_index == slot), 1.0, 0.0),
+        jnp.where(alive, 0.0, 1.0),
+    ).astype(BF16)
+    query_lane = lax.broadcasted_iota(jnp.int32, (slab, channels), 1)
+    query_map = jnp.where(
+        (query_lane // band == token_col.astype(jnp.int32)) | (query_lane == dead_lane), 1.0, 0.0
+    )
+    score_row = lax.broadcasted_iota(jnp.int32, (slab, ext), 0) // QUERY_WINDOW * QUERY_WINDOW
+    score_lane = lax.broadcasted_iota(jnp.int32, (slab, ext), 1)
+    in_window = (score_lane >= score_row) & (score_lane < score_row + KEYS)
+
+    pltpu.make_async_copy(send_sums.at[others], recv_sums.at[others], recv_sem.at[1]).wait()
+    sums_wide[...] = recv_sums[...].reshape(devices * block, tokens).astype(F32)
+    band_row = lax.broadcasted_iota(jnp.int32, (band, tokens), 0)
+    band_lane = lax.broadcasted_iota(jnp.int32, (band, tokens), 1)
+    selector = jnp.where(
+        (band_lane == (me - 1) * tok_rows + band_row) & (band_row < 3 * tok_rows), 1.0, 0.0
+    ).astype(BF16)
+    bands = []
+    for i in range(tok_rows):
+        merged = jnp.concatenate(
+            [
+                sums_wide[pl.ds(i * owned + c, devices, stride=block), :]
+                for c in range(owned)
+            ],
+            axis=0,
+        )
+        tri_norm = normed(merged, 0).T.astype(BF16)
+        update = dot_nn(tri_norm, tri_out_weight[...])
+        updated = (pair[i].astype(F32) + gate_ref[i] * update).astype(BF16)
+        pair_out[i] = updated
+        bands.append(dot_nn(selector, updated))
+    bands.append(jnp.zeros((channels - tok_rows * band, channels), F32))
+    band_norm = normed(jnp.concatenate(bands, axis=0), 1).astype(BF16)
+    table = dot_nt(bias_weight[...].astype(F32).T.astype(BF16), band_norm).astype(BF16).astype(F32)
+    table_lane = lax.broadcasted_iota(jnp.int32, table.shape, 1)
+    table = jnp.where(table_lane == dead_lane, -1e30, table)
+    bias_rows = jnp.concatenate(
+        [query_map * table[h : h + 1] for h in range(heads)], axis=0
+    ).astype(BF16)
+    scores = raw_scores + dot_nt(bias_rows, key_map)
+    scores = jnp.where(jnp.concatenate([in_window] * heads, axis=0), scores, -1e30)
+    scores = jnp.exp(scores - jnp.max(scores, axis=1, keepdims=True))
+    weights = (scores / jnp.sum(scores, axis=1, keepdims=True)).astype(BF16)
+    mixed = dot_nn(weights, values)
+    attended = jnp.zeros((slab, width), F32)
+    for h in range(heads):
+        attended = jnp.where(head_lane == h, mixed[h * slab : (h + 1) * slab], attended)
+    atom_mid = act + dot_nn(attended.astype(BF16), attn_out_weight[...])
+    expanded = dot_nn(normed(atom_mid, 1).astype(BF16), ffn_in_weight[...])
+    hidden = ffn_out_weight.shape[0]
+    up_part, gate_part = expanded[:, hidden:], expanded[:, :hidden]
+    inner = (gate_part * jax.nn.sigmoid(gate_part) * up_part).astype(BF16)
+    result = ((atom_mid + dot_nn(inner, ffn_out_weight[...])) * live_col).astype(BF16)
+    atom_out[...] = result
+    features = jnp.maximum(dot_nn(result, agg_weight[...]), 0.0).astype(BF16)
+    owner_row = lax.broadcasted_iota(jnp.int32, (tok_rows, slab), 0)
+    owner = jnp.where((owner_row == token_row) & (live_row > 0), 1.0, 0.0)
+    counts = jnp.sum(owner, axis=1, keepdims=True)
+    token_out[...] = (dot_nn(owner.astype(BF16), features) / counts).astype(BF16)
+
+    pltpu.make_async_copy(send_terms.at[others], recv_terms.at[others], send_sem.at[0]).wait()
+    pltpu.make_async_copy(send_sums.at[others], recv_sums.at[others], send_sem.at[1]).wait()
+
+    @pl.when(me < devices - 1)
+    def _():
+        up.wait_send()
+
+    @pl.when(me > 0)
+    def _():
+        down.wait_send()
+
+
+def per_device(*args):
+    pair, token_mask, atom_act, atom_token = args[0], args[1], args[5], args[7]
+    tok_rows, tokens, channels = pair.shape
+    slab, width = atom_act.shape
+    heads = args[11].shape[1]
+    devices = lax.axis_size("row")
+    owned = channels // devices
+    block = tok_rows * owned
+    fits = (
+        lax.axis_size("col") == 1
+        and owned * devices == channels
+        and block % 16 == 0
+        and slab % QUERY_WINDOW == 0
+        and devices % 8 == 0
+        and width == channels
+        and 4 * tok_rows % 16 == 0
+        and 4 * tok_rows * tok_rows < channels
+        and slab >= (KEYS - QUERY_WINDOW) // 2
+    )
+    if not fits:
+        return spread_device(*args)
+    side = (KEYS - QUERY_WINDOW) // 2
+    args = list(args)
+    for k in (1, 7, 8):
+        args[k] = args[k].reshape(1, -1)
+    agg_width = args[15].shape[1]
+    sizes = (devices, tok_rows, tokens, channels, owned, slab, heads)
+    in_vmem = pl.BlockSpec(memory_space=pltpu.VMEM)
+    return tuple(
+        pl.pallas_call(
+            functools.partial(fused_kernel, sizes),
+            out_shape=(
+                jax.ShapeDtypeStruct(pair.shape, BF16),
+                jax.ShapeDtypeStruct(atom_act.shape, BF16),
+                jax.ShapeDtypeStruct((tok_rows, agg_width), BF16),
+            ),
+            in_specs=[in_vmem] * len(args),
+            out_specs=(in_vmem,) * 3,
+            scratch_shapes=[
+                pltpu.VMEM((2, devices * block, tokens), F32),
+                pltpu.VMEM((devices, 2, block, tokens), BF16),
+                pltpu.VMEM((devices, 2, block, tokens), BF16),
+                pltpu.VMEM((devices * block, tokens), F32),
+                pltpu.VMEM((devices * block, tokens), F32),
+                pltpu.VMEM((devices * block, tokens), F32),
+                pltpu.VMEM((devices, block, tokens), BF16),
+                pltpu.VMEM((devices, block, tokens), BF16),
+                pltpu.VMEM((tok_rows, tokens, channels), F32),
+                pltpu.VMEM((slab + 2 * side, 3 * width), BF16),
+                pltpu.SemaphoreType.DMA((2,)),
+                pltpu.SemaphoreType.DMA((2,)),
+                pltpu.SemaphoreType.DMA((2,)),
+                pltpu.SemaphoreType.DMA((2,)),
+            ],
+            compiler_params=pltpu.CompilerParams(
+                collective_id=0, has_side_effects=True, vmem_limit_bytes=32 * 1024 * 1024
+            ),
+            name="triangle_atoms",
+        )(*args)
+    )
+
+
 def solution(mesh):
     in_specs = (
         P(("groups", "row"), "col", None),

time: 61.9 us -> 35.7 us (0.58)
  starting transfers between devices: 28.7 us -> 0 us
  Pallas kernels: 0 us -> 22.5 us
  waiting for transfers between devices: 12 us -> 0 us
  matrix products: 4.74 us -> 0 us
  other arithmetic: 3.08 us -> 0 us
    pallas_call x0 -> x1, Pallas kernels: none -> 22.5 us  [per_device(): pl.pallas_call(functools.partial(fused_kernel, sizes), out_shape=(jax.Sha...]
    all_to_all x3 -> x0, starting transfers between devices: 19.8 us -> none  [the longest x1 9.8 us: per_device(): lax.all_to_all(left, 'row', split_axis=0, concat_axis=1, tiled=True)]
    all_to_all x3 -> x0, waiting for transfers between devices: 12 us -> none  [the longest x1 6.74 us: per_device(): lax.all_to_all(tri_sum, 'row', split_axis=1, concat_axis=0, tiled=True)]
    ppermute x4 -> x0, starting transfers between devices: 8.9 us -> none  [the longest x2 6.31 us: extended(): before = lax.ppermute(last, axis, up)]
    unnamed x40 -> x34, local copies, waits for them, and re-layouts: 4.36 us -> 11.8 us
    dot_general x17 -> x0, matrix products: 4.74 us -> none  [the longest x1 0.85 us: per_device(): jnp.einsum('at,ac->tc', live_onehot, features, preferred_element_type=jnp...]
    gather x3 -> x0, local copies, waits for them, and re-layouts: 3.84 us -> none  [the longest x1 1.88 us: per_device(): window_valid = key_valid[key_index]]
    convert_element_type x6 -> x0, local copies, waits for them, and re-layouts: 2.58 us -> none  [the longest x1 0.79 us: per_device(): (jax.nn.sigmoid(left_terms[channels:]) * left_terms[:channels] * pair_liv...]
  transfers between devices with their start and end apart: 7 -> 0, of which waited for: 2 -> 0; matrix products, arithmetic and copies ran while one was open for 13% -> 0% of each run, Pallas kernels for 0% -> 0%
where the time goes in v1:
time: 35.7 us; the launch traced here: 35 us
  Pallas kernels  22.5 us (63%)
  local copies, waits for them, and re-layouts  11.8 us (33%)
  between operations  0.71 us (2%)
    pallas_call x1, Pallas kernels, per_device(): pl.pallas_call(functools.partial(fused_kernel, sizes), out_shape=(jax.Sha...  22.5 us
    unnamed x34, local copies, waits for them, and re-layouts  11.8 us

profile of v1, /device:TPU:0, one launch (start us, length us, event | category | flops | bytes accessed | tf_op | source)
XLA Modules:
  0.0 35.0 jit_solution(296898266515129123)
XLA Ops:
  0.6 0.0 copy-start.7
  0.6 0.0 copy-start.12
  0.7 0.0 copy-start.13
  0.7 0.0 copy-start.14
  0.7 0.8 %copy.19.bias_weight = bf16[128,4]{1,0:T(8,128)(2,1)S(1)} copy(bf16[128,4]{0,1:T(4,128)(2,1)} %param.27) | data formatting | bytes 2048 | tf_op args[11]
  1.5 0.0 copy-done.7
  1.5 0.0 copy-done.13
  1.5 0.0 copy-done.14
  1.5 0.0 copy-start
  1.5 0.9 %copy-done = bf16[4,128,128]{2,1,0:T(8,128)(2,1)S(1)} copy-done((bf16[4,128,128]{2,1,0:T(8,128)(2,1)S(1)}, bf16[4,128,128]{2,1,0:T(8,128)(2,1)}, u32[]{:S(2)}) %copy-start) | copy-done | bytes 131096
  2.4 0.9 %copy-done.1 = bf16[128,512]{1,0:T(8,128)(2,1)S(1)} copy-done((bf16[128,512]{1,0:T(8,128)(2,1)S(1)}, bf16[128,512]{1,0:T(8,128)(2,1)}, u32[]{:S(2)}) %copy-start.1) | copy-done | bytes 131096
  3.3 0.9 %copy-done.2 = bf16[128,512]{1,0:T(8,128)(2,1)S(1)} copy-done((bf16[128,512]{1,0:T(8,128)(2,1)S(1)}, bf16[128,512]{1,0:T(8,128)(2,1)}, u32[]{:S(2)}) %copy-start.2) | copy-done | bytes 131096
  4.3 0.9 %copy-done.3 = bf16[128,384]{1,0:T(8,128)(2,1)S(1)} copy-done((bf16[128,384]{1,0:T(8,128)(2,1)S(1)}, bf16[128,384]{1,0:T(8,128)(2,1)}, u32[]{:S(2)}) %copy-start.3) | copy-done | bytes 98328
  5.1 0.9 %copy-done.4 = bf16[128,384]{1,0:T(8,128)(2,1)S(1)} copy-done((bf16[128,384]{1,0:T(8,128)(2,1)S(1)}, bf16[128,384]{1,0:T(8,128)(2,1)}, u32[]{:S(2)}) %copy-start.4) | copy-done | bytes 98328
  6.0 0.8 %copy-done.5 = bf16[128,256]{1,0:T(8,128)(2,1)S(1)} copy-done((bf16[128,256]{1,0:T(8,128)(2,1)S(1)}, bf16[128,256]{1,0:T(8,128)(2,1)}, u32[]{:S(2)}) %copy-start.5) | copy-done | bytes 65560
  6.9 0.8 %copy-done.6 = bf16[256,128]{1,0:T(8,128)(2,1)S(1)} copy-done((bf16[256,128]{1,0:T(8,128)(2,1)S(1)}, bf16[256,128]{1,0:T(8,128)(2,1)}, u32[]{:S(2)}) %copy-start.6) | copy-done | bytes 65560
  7.7 0.8 %copy-done.8 = bf16[128,128]{1,0:T(8,128)(2,1)S(1)} copy-done((bf16[128,128]{1,0:T(8,128)(2,1)S(1)}, bf16[128,128]{1,0:T(8,128)(2,1)}, u32[]{:S(2)}) %copy-start.8) | copy-done | bytes 32792
  8.5 0.8 %copy-done.9 = bf16[128,128]{1,0:T(8,128)(2,1)S(1)} copy-done((bf16[128,128]{1,0:T(8,128)(2,1)S(1)}, bf16[128,128]{1,0:T(8,128)(2,1)}, u32[]{:S(2)}) %copy-start.9) | copy-done | bytes 32792
  9.2 0.7 %copy-done.10 = bf16[64,128]{1,0:T(8,128)(2,1)S(1)} copy-done((bf16[64,128]{1,0:T(8,128)(2,1)S(1)}, bf16[64,128]{1,0:T(8,128)(2,1)}, u32[]{:S(2)}) %copy-start.10) | copy-done | bytes 16408
  10.0 0.7 %copy-done.11 = bf16[64,128]{1,0:T(8,128)(2,1)S(1)} copy-done((bf16[64,128]{1,0:T(8,128)(2,1)S(1)}, bf16[64,128]{1,0:T(8,128)(2,1)}, u32[]{:S(2)}) %copy-start.11) | copy-done | bytes 16408
  10.7 22.5 %triangle_atoms.1 = (bf16[4,128,128]{2,1,0:T(8,128)(2,1)S(1)}, bf16[64,128]{1,0:T(8,128)(2,1)S(1)}, bf16[4,384]{1,0:T(4,128)(2,1)S(1)}) custom-call(bf16[4,128,128]{2,1,0:T(8,128)(2,1)S(1)} %copy-done, s32[1,128]{1,0:T(1,128)S(1)} %bitcast.3, bf16[128,512]{1,0:T(8,128)(2,1)S(1)} %copy-done.1, bf16[128,128]{1,0:T(8,128)(2,1)S(1)} %copy-done.7, ...), custom_call_target="tpu_custom_call" | custom-call | tf_op jit(solution)/shard_map/triangle_atoms/pallas_call | solution.py:531
  33.2 0.7 %copy.23 = bf16[4,128,128]{2,1,0:T(8,128)(2,1)} copy(bf16[4,128,128]{2,1,0:T(8,128)(2,1)S(1)} %get-tuple-element.6) | data formatting | bytes 262144
  33.9 0.6 %copy.24 = bf16[64,128]{1,0:T(8,128)(2,1)} copy(bf16[64,128]{1,0:T(8,128)(2,1)S(1)} %get-tuple-element.7) | data formatting | bytes 32768
  34.5 0.6 %copy.25 = bf16[4,384]{1,0:T(4,128)(2,1)} copy(bf16[4,384]{1,0:T(4,128)(2,1)S(1)} %get-tuple-element.8) | data formatting | bytes 6144
  (11 shorter events, 0.0 us)
Async XLA Ops:
  0.6 0.9 %copy-start.7 = (bf16[128,128]{1,0:T(8,128)(2,1)S(1)}, bf16[128,128]{1,0:T(8,128)(2,1)}, u32[]{:S(2)}) copy-start(bf16[128,128]{1,0:T(8,128)(2,1)} %tri_gate_weight.1) | copy-start | bytes 98308
  0.6 0.9 %copy-start.12 = (s32[128]{0:T(128)S(1)}, s32[128]{0:T(128)}, u32[]{:S(2)}) copy-start(s32[128]{0:T(128)} %param.17) | copy-start | bytes 1540
  0.7 0.9 %copy-start.13 = (s32[64]{0:T(128)S(1)}, s32[64]{0:T(128)}, u32[]{:S(2)}) copy-start(s32[64]{0:T(128)} %param.23) | copy-start | bytes 772
  0.7 0.9 %copy-start.14 = (s32[64]{0:T(128)S(1)}, s32[64]{0:T(128)}, u32[]{:S(2)}) copy-start(s32[64]{0:T(128)} %param.24) | copy-start | bytes 772
  1.5 0.9 %copy-start = (bf16[4,128,128]{2,1,0:T(8,128)(2,1)S(1)}, bf16[4,128,128]{2,1,0:T(8,128)(2,1)}, u32[]{:S(2)}) copy-start(bf16[4,128,128]{2,1,0:T(8,128)(2,1)} %pair.1) | copy-start | bytes 393220
  2.4 0.9 %copy-start.1 = (bf16[128,512]{1,0:T(8,128)(2,1)S(1)}, bf16[128,512]{1,0:T(8,128)(2,1)}, u32[]{:S(2)}) copy-start(bf16[128,512]{1,0:T(8,128)(2,1)} %tri_in_weight.1) | copy-start | bytes 393220
  3.3 0.9 %copy-start.2 = (bf16[128,512]{1,0:T(8,128)(2,1)S(1)}, bf16[128,512]{1,0:T(8,128)(2,1)}, u32[]{:S(2)}) copy-start(bf16[128,512]{1,0:T(8,128)(2,1)} %ffn_in_weight.1) | copy-start | bytes 393220
  4.3 0.9 %copy-start.3 = (bf16[128,384]{1,0:T(8,128)(2,1)S(1)}, bf16[128,384]{1,0:T(8,128)(2,1)}, u32[]{:S(2)}) copy-start(bf16[128,384]{1,0:T(8,128)(2,1)} %qkv_weight.1) | copy-start | bytes 294916
  5.1 0.9 %copy-start.4 = (bf16[128,384]{1,0:T(8,128)(2,1)S(1)}, bf16[128,384]{1,0:T(8,128)(2,1)}, u32[]{:S(2)}) copy-start(bf16[128,384]{1,0:T(8,128)(2,1)} %agg_weight.1) | copy-start | bytes 294916
  6.0 0.8 %copy-start.5 = (bf16[128,256]{1,0:T(8,128)(2,1)S(1)}, bf16[128,256]{1,0:T(8,128)(2,1)}, u32[]{:S(2)}) copy-start(bf16[128,256]{1,0:T(8,128)(2,1)} %ada_weight.1) | copy-start | bytes 196612
  6.9 0.8 %copy-start.6 = (bf16[256,128]{1,0:T(8,128)(2,1)S(1)}, bf16[256,128]{1,0:T(8,128)(2,1)}, u32[]{:S(2)}) copy-start(bf16[256,128]{1,0:T(8,128)(2,1)} %ffn_out_weight.1) | copy-start | bytes 196612
  7.7 0.8 %copy-start.8 = (bf16[128,128]{1,0:T(8,128)(2,1)S(1)}, bf16[128,128]{1,0:T(8,128)(2,1)}, u32[]{:S(2)}) copy-start(bf16[128,128]{1,0:T(8,128)(2,1)} %tri_out_weight.1) | copy-start | bytes 98308
  8.5 0.8 %copy-start.9 = (bf16[128,128]{1,0:T(8,128)(2,1)S(1)}, bf16[128,128]{1,0:T(8,128)(2,1)}, u32[]{:S(2)}) copy-start(bf16[128,128]{1,0:T(8,128)(2,1)} %attn_out_weight.1) | copy-start | bytes 98308
  9.2 0.7 %copy-start.10 = (bf16[64,128]{1,0:T(8,128)(2,1)S(1)}, bf16[64,128]{1,0:T(8,128)(2,1)}, u32[]{:S(2)}) copy-start(bf16[64,128]{1,0:T(8,128)(2,1)} %atom_act.1) | copy-start | bytes 49156
  10.0 0.7 %copy-start.11 = (bf16[64,128]{1,0:T(8,128)(2,1)S(1)}, bf16[64,128]{1,0:T(8,128)(2,1)}, u32[]{:S(2)}) copy-start(bf16[64,128]{1,0:T(8,128)(2,1)} %atom_cond.1) | copy-start | bytes 49156

commit v2 on v1

--- a/solution.py
+++ b/solution.py
@@ -227,42 +227,59 @@
     return centred * lax.rsqrt(spread + EPSILON)
 
 
+FETCH_ORDER = (0, 2, 1, 3, 6, 9, 5, 7, 8, 10, 4, 11, 12, 13, 14, 15)
+
+
 def fused_kernel(
     sizes,
-    pair,
-    token_mask,
-    tri_in_weight,
-    tri_gate_weight,
-    tri_out_weight,
-    atom_act,
-    atom_cond,
-    atom_token,
-    atom_mask,
-    ada_weight,
-    qkv_weight,
-    bias_weight,
-    attn_out_weight,
-    ffn_in_weight,
-    ffn_out_weight,
-    agg_weight,
-    pair_out,
-    atom_out,
-    token_out,
-    terms_wide,
-    send_terms,
-    recv_terms,
-    left_wide,
-    right_wide,
-    sums_wide,
-    send_sums,
-    recv_sums,
-    gate_ref,
-    rim,
-    send_sem,
-    recv_sem,
-    rim_send,
-    rim_recv,
+    *refs,
 ):
+    count = len(FETCH_ORDER)
+    operands, refs = refs[:count], refs[count:]
+    (
+        pair_out,
+        atom_out,
+        token_out,
+        terms_wide,
+        send_terms,
+        recv_terms,
+        left_wide,
+        right_wide,
+        sums_wide,
+        send_sums,
+        recv_sums,
+        gate_ref,
+        rim,
+        send_sem,
+        recv_sem,
+        rim_send,
+        rim_recv,
+        fetch_sem,
+    ) = refs[: len(refs) - count]
+    held = refs[len(refs) - count :]
+    fetches = [
+        pltpu.make_async_copy(operands[k], held[k], fetch_sem.at[k]) for k in range(count)
+    ]
+    for k in FETCH_ORDER:
+        fetches[k].start()
+    (
+        pair,
+        token_mask,
+        tri_in_weight,
+        tri_gate_weight,
+        tri_out_weight,
+        atom_act,
+        atom_cond,
+        atom_token,
+        atom_mask,
+        ada_weight,
+        qkv_weight,
+        bias_weight,
+        attn_out_weight,
+        ffn_in_weight,
+        ffn_out_weight,
+        agg_weight,
+    ) = held
     devices, tok_rows, tokens, channels, owned, slab, heads = sizes
     block = tok_rows * owned
     side = (KEYS - QUERY_WINDOW) // 2
@@ -280,6 +297,8 @@
 
     lax.fori_loop(1, devices, greet, 0)
 
+    for k in (0, 2, 1, 3):
+        fetches[k].wait()
     mask_row = token_mask[...].astype(F32)
     lane = lax.broadcasted_iota(jnp.int32, (1, tokens), 1)
     in_weight = tri_in_weight[...].T
@@ -322,6 +341,8 @@
     lax.fori_loop(1, devices, send_first, 0)
     recv_terms[me] = send_terms[me]
 
+    for k in (6, 9, 5, 7, 8, 10):
+        fetches[k].wait()
     token_row = atom_token[...] - me * tok_rows
     live_row = atom_mask[...]
     wide = (channels, slab)
@@ -437,6 +458,8 @@
     score_lane = lax.broadcasted_iota(jnp.int32, (slab, ext), 1)
     in_window = (score_lane >= score_row) & (score_lane < score_row + KEYS)
 
+    for k in (4, 11, 12, 13, 14, 15):
+        fetches[k].wait()
     pltpu.make_async_copy(send_sums.at[others], recv_sums.at[others], recv_sem.at[1]).wait()
     sums_wide[...] = recv_sums[...].reshape(devices * block, tokens).astype(F32)
     band_row = lax.broadcasted_iota(jnp.int32, (band, tokens), 0)
@@ -460,7 +483,7 @@
         bands.append(dot_nn(selector, updated))
     bands.append(jnp.zeros((channels - tok_rows * band, channels), F32))
     band_norm = normed(jnp.concatenate(bands, axis=0), 1).astype(BF16)
-    table = dot_nt(bias_weight[...].astype(F32).T.astype(BF16), band_norm).astype(BF16).astype(F32)
+    table = dot_nt(bias_weight[...], band_norm).astype(BF16).astype(F32)
     table_lane = lax.broadcasted_iota(jnp.int32, table.shape, 1)
     table = jnp.where(table_lane == dead_lane, -1e30, table)
     bias_rows = jnp.concatenate(
@@ -524,9 +547,11 @@
     args = list(args)
     for k in (1, 7, 8):
         args[k] = args[k].reshape(1, -1)
+    args[11] = args[11].T
     agg_width = args[15].shape[1]
     sizes = (devices, tok_rows, tokens, channels, owned, slab, heads)
     in_vmem = pl.BlockSpec(memory_space=pltpu.VMEM)
+    in_hbm = pl.BlockSpec(memory_space=pltpu.HBM)
     return tuple(
         pl.pallas_call(
             functools.partial(fused_kernel, sizes),
@@ -535,7 +560,7 @@
                 jax.ShapeDtypeStruct(atom_act.shape, BF16),
                 jax.ShapeDtypeStruct((tok_rows, agg_width), BF16),
             ),
-            in_specs=[in_vmem] * len(args),
+            in_specs=[in_hbm] * len(args),
             out_specs=(in_vmem,) * 3,
             scratch_shapes=[
                 pltpu.VMEM((2, devices * block, tokens), F32),
@@ -552,9 +577,11 @@
                 pltpu.SemaphoreType.DMA((2,)),
                 pltpu.SemaphoreType.DMA((2,)),
                 pltpu.SemaphoreType.DMA((2,)),
+                pltpu.SemaphoreType.DMA((len(args),)),
+                *[pltpu.VMEM(a.shape, a.dtype) for a in args],
             ],
             compiler_params=pltpu.CompilerParams(
-                collective_id=0, has_side_effects=True, vmem_limit_bytes=32 * 1024 * 1024
+                collective_id=0, has_side_effects=True, vmem_limit_bytes=60 * 1024 * 1024
             ),
             name="triangle_atoms",
         )(*args)

time: 35.7 us -> 27 us (0.76); the launches traced: 35 us -> 26.8 us
  local copies, waits for them, and re-layouts: 11.8 us -> 2.82 us
  Pallas kernels: 22.5 us -> 23.4 us
    unnamed x34 -> x7, local copies, waits for them, and re-layouts: 11.8 us -> 2.82 us
    pallas_call x1, Pallas kernels: 22.5 us -> 23.4 us  [per_device(): pl.pallas_call(functools.partial(fused_kernel, sizes), out_shape=(jax.Sha...]
where the time goes in v2:
time: 27 us; the launch traced here: 26.8 us
  Pallas kernels  23.4 us (87%)
  local copies, waits for them, and re-layouts  2.82 us (10%)
  between operations  0.66 us (2%)
    pallas_call x1, Pallas kernels, per_device(): pl.pallas_call(functools.partial(fused_kernel, sizes), out_shape=(jax.Sha...  23.4 us
    unnamed x7, local copies, waits for them, and re-layouts  2.82 us

profile of v2, /device:TPU:0, one launch (start us, length us, event | category | flops | bytes accessed | tf_op | source)
XLA Modules:
  0.0 26.8 jit_solution(7979739933869821432)
XLA Ops:
  0.6 23.4 %triangle_atoms.1 = (bf16[4,128,128]{2,1,0:T(8,128)(2,1)}, bf16[64,128]{1,0:T(8,128)(2,1)}, bf16[4,384]{1,0:T(4,128)(2,1)}) custom-call(bf16[4,128,128]{2,1,0:T(8,128)(2,1)} %refs_0_.1, s32[1,128]{1,0:T(1,128)} %bitcast.5, bf16[128,512]{1,0:T(8,128)(2,1)} %refs_2_.1, bf16[128,128]{1,0:T(8,128)(2,1)} %refs_3_.1, bf16[128,128]{1,0:T(8,128)(2,1)} %refs_4_.1, ...), custom_call_target="tpu_custom_call" | custom-call | tf_op jit(solution)/shard_map/triangle_atoms/pallas_call | solution.py:556
  24.0 0.0 copy-start
  24.0 1.6 %copy.22 = bf16[4,128,128]{2,1,0:T(8,128)(2,1)} copy(bf16[4,128,128]{2,1,0:T(8,128)(2,1)} %get-tuple-element.6) | data formatting | bytes 262144
  25.6 0.0 copy-done
  25.6 0.0 copy-start.1
  25.6 0.6 %copy.23 = bf16[64,128]{1,0:T(8,128)(2,1)} copy(bf16[64,128]{1,0:T(8,128)(2,1)S(1)} %copy-done) | data formatting | bytes 32768
  26.2 0.1 copy-done.1
  26.3 0.6 %copy.24 = bf16[4,384]{1,0:T(4,128)(2,1)} copy(bf16[4,384]{1,0:T(4,128)(2,1)S(1)} %copy-done.1) | data formatting | bytes 6144
Async XLA Ops:
  24.0 1.6 %copy-start = (bf16[64,128]{1,0:T(8,128)(2,1)S(1)}, bf16[64,128]{1,0:T(8,128)(2,1)}, u32[]{:S(2)}) copy-start(bf16[64,128]{1,0:T(8,128)(2,1)} %get-tuple-element.7) | copy-start | bytes 49156
  25.6 0.7 %copy-start.1 = (bf16[4,384]{1,0:T(4,128)(2,1)S(1)}, bf16[4,384]{1,0:T(4,128)(2,1)}, u32[]{:S(2)}) copy-start(bf16[4,384]{1,0:T(4,128)(2,1)} %get-tuple-element.8) | copy-start | bytes 9220

commit v3 on v2

--- a/solution.py
+++ b/solution.py
@@ -556,9 +556,9 @@
         pl.pallas_call(
             functools.partial(fused_kernel, sizes),
             out_shape=(
-                jax.ShapeDtypeStruct(pair.shape, BF16),
-                jax.ShapeDtypeStruct(atom_act.shape, BF16),
-                jax.ShapeDtypeStruct((tok_rows, agg_width), BF16),
+                pltpu.VMEM(pair.shape, BF16),
+                pltpu.VMEM(atom_act.shape, BF16),
+                pltpu.VMEM((tok_rows, agg_width), BF16),
             ),
             in_specs=[in_hbm] * len(args),
             out_specs=(in_vmem,) * 3,

time: 27 us -> 25.4 us (0.941)
  local copies, waits for them, and re-layouts: 2.82 us -> 1.84 us
  Pallas kernels: 23.4 us -> 22.7 us
    unnamed x7 -> x3, local copies, waits for them, and re-layouts: 2.82 us -> 1.84 us
    pallas_call x1, Pallas kernels: 23.4 us -> 22.7 us  [per_device(): pl.pallas_call(functools.partial(fused_kernel, sizes), out_shape=(pltpu.V...]
where the time goes in v3:
time: 25.4 us; the launch traced here: 25.2 us
  Pallas kernels  22.7 us (89%)
  local copies, waits for them, and re-layouts  1.84 us (7%)
  between operations  0.65 us (3%)
    pallas_call x1, Pallas kernels, per_device(): pl.pallas_call(functools.partial(fused_kernel, sizes), out_shape=(pltpu.V...  22.7 us
    unnamed x3, local copies, waits for them, and re-layouts  1.84 us

profile of v3, /device:TPU:0, one launch (start us, length us, event | category | flops | bytes accessed | tf_op | source)
XLA Modules:
  0.0 25.2 jit_solution(3876056954704242258)
XLA Ops:
  0.6 22.7 %triangle_atoms.1 = (bf16[4,128,128]{2,1,0:T(8,128)(2,1)S(1)}, bf16[64,128]{1,0:T(8,128)(2,1)S(1)}, bf16[4,384]{1,0:T(4,128)(2,1)S(1)}) custom-call(bf16[4,128,128]{2,1,0:T(8,128)(2,1)} %refs_0_.1, s32[1,128]{1,0:T(1,128)} %bitcast.5, bf16[128,512]{1,0:T(8,128)(2,1)} %refs_2_.1, bf16[128,128]{1,0:T(8,128)(2,1)} %refs_3_.1, bf16[128,128]{1,0:T(8,128)(2,1)} %refs_4_.1, ...), custom_call_target="tpu_custom_call" | custom-call | tf_op jit(solution)/shard_map/triangle_atoms/pallas_call | solution.py:556
  23.4 0.7 %copy.22 = bf16[4,128,128]{2,1,0:T(8,128)(2,1)} copy(bf16[4,128,128]{2,1,0:T(8,128)(2,1)S(1)} %get-tuple-element.3) | data formatting | bytes 262144
  24.0 0.6 %copy.24 = bf16[4,384]{1,0:T(4,128)(2,1)} copy(bf16[4,384]{1,0:T(4,128)(2,1)S(1)} %get-tuple-element.5) | data formatting | bytes 6144
  24.6 0.6 %copy.23 = bf16[64,128]{1,0:T(8,128)(2,1)} copy(bf16[64,128]{1,0:T(8,128)(2,1)S(1)} %get-tuple-element.4) | data formatting | bytes 32768

commit v4 on v3

--- a/solution.py
+++ b/solution.py
@@ -334,11 +334,13 @@
             device_id_type=MESH,
         )
 
-    def send_first(step, carry):
-        terms_copy(lax.rem(me + step, devices)).start()
+    def send_first(pair_step, carry):
+        terms_copy(lax.rem(me + pair_step, devices)).start()
+        terms_copy(lax.rem(me + devices - pair_step, devices)).start()
         return carry
 
-    lax.fori_loop(1, devices, send_first, 0)
+    lax.fori_loop(1, devices // 2, send_first, 0)
+    terms_copy(lax.rem(me + devices // 2, devices)).start()
     recv_terms[me] = send_terms[me]
 
     for k in (6, 9, 5, 7, 8, 10):
@@ -410,11 +412,13 @@
             device_id_type=MESH,
         )
 
-    def send_second(step, carry):
-        sums_copy(lax.rem(me + step, devices)).start()
+    def send_second(pair_step, carry):
+        sums_copy(lax.rem(me + pair_step, devices)).start()
+        sums_copy(lax.rem(me + devices - pair_step, devices)).start()
         return carry
 
-    lax.fori_loop(1, devices, send_second, 0)
+    lax.fori_loop(1, devices // 2, send_second, 0)
+    sums_copy(lax.rem(me + devices // 2, devices)).start()
     recv_sums[me] = send_sums[me]
 
     @pl.when(me > 0)

time: 25.4 us -> 25.2 us (level)
  no operation moved by 1% of the time
where the time goes in v4:
time: 25.2 us; the launch traced here: 25 us
  Pallas kernels  22.5 us (89%)
  local copies, waits for them, and re-layouts  1.84 us (7%)
  between operations  0.65 us (3%)
    pallas_call x1, Pallas kernels, per_device(): pl.pallas_call(functools.partial(fused_kernel, sizes), out_shape=(pltpu.V...  22.5 us
    unnamed x3, local copies, waits for them, and re-layouts  1.84 us

profile of v4, /device:TPU:0, one launch (start us, length us, event | category | flops | bytes accessed | tf_op | source)
XLA Modules:
  0.0 25.0 jit_solution(16905257049392778738)
XLA Ops:
  0.6 22.5 %triangle_atoms.1 = (bf16[4,128,128]{2,1,0:T(8,128)(2,1)S(1)}, bf16[64,128]{1,0:T(8,128)(2,1)S(1)}, bf16[4,384]{1,0:T(4,128)(2,1)S(1)}) custom-call(bf16[4,128,128]{2,1,0:T(8,128)(2,1)} %refs_0_.1, s32[1,128]{1,0:T(1,128)} %bitcast.5, bf16[128,512]{1,0:T(8,128)(2,1)} %refs_2_.1, bf16[128,128]{1,0:T(8,128)(2,1)} %refs_3_.1, bf16[128,128]{1,0:T(8,128)(2,1)} %refs_4_.1, ...), custom_call_target="tpu_custom_call" | custom-call | tf_op jit(solution)/shard_map/triangle_atoms/pallas_call | solution.py:560
  23.2 0.7 %copy.22 = bf16[4,128,128]{2,1,0:T(8,128)(2,1)} copy(bf16[4,128,128]{2,1,0:T(8,128)(2,1)S(1)} %get-tuple-element.3) | data formatting | bytes 262144
  23.8 0.6 %copy.24 = bf16[4,384]{1,0:T(4,128)(2,1)} copy(bf16[4,384]{1,0:T(4,128)(2,1)S(1)} %get-tuple-element.5) | data formatting | bytes 6144
  24.4 0.6 %copy.23 = bf16[64,128]{1,0:T(8,128)(2,1)} copy(bf16[64,128]{1,0:T(8,128)(2,1)S(1)} %get-tuple-element.4) | data formatting | bytes 32768
